TPU v7x, 32 devices: a whole 2x2x4 slice. The times are simulated.
32 devices in a mesh: ga: 32 (over z, y, x, core), gp: 1.
Axes of the slice: x: 2, y: 2, z: 4, core: 2. Of those that a mesh axis runs over, the one named last changes fastest.
Arguments:
- screened: bfloat16 [8192, 65536], P('ga', 'gp'), may hold values from -0.0234375 to 0.0234375
- valence: bfloat16 [32, 32, 65536], P('ga', None, 'gp'), may hold values from -6 to 6
- conduction: bfloat16 [1024, 8192], P(None, 'ga'), may hold values from -0.125 to 0.125
- owner: int32 [6], replicated, may hold values from 0 to 31
Outputs:
- kernel: float32 [1024, 192], P('ga', 'gp')
Inputs may be any that keep to these rules, and one draw needn't show every extreme that they name: owner[b] is the slot of valence, along its first dimension, that holds batch b.
All inputs are finite; a program needn't handle non-finite values.
Results may differ from a plain program's by a relative error of at most 0.0003.
Values may be sent and summed in bfloat16 or wider, within the bound.
A program may use at most 128 MiB of HBM per device.

v0:
```python
import jax
import jax.numpy as jnp
from jax import lax
from jax.sharding import PartitionSpec as P


def spread(block, axis, source):
    block = jnp.where(lax.axis_index(axis) == source, block, jnp.zeros_like(block))
    return lax.psum(block, axis)


def body(screened, valence, conduction, owner):
    own_slot = valence[0]
    dims = (((1,), (1,)), ((), ()))
    pieces = []
    for batch in range(owner.shape[0]):
        chosen = spread(own_slot, "ga", owner[batch])
        pieces.append(lax.dot_general(screened, chosen, dims, preferred_element_type=jnp.float32))
    partial_value = jnp.concatenate(pieces, axis=1)
    cond_full = conduction.astype(jnp.float32)
    term = jnp.dot(cond_full, partial_value, precision=lax.Precision.HIGHEST)
    columns = lax.psum_scatter(term, "gp", scatter_dimension=1, tiled=True)
    kernel = lax.psum_scatter(columns, "ga", scatter_dimension=0, tiled=True)
    return kernel


def solution(mesh):
    placed = (P("ga", "gp"), P("ga", None, "gp"), P(None, "ga"), P())
    return jax.shard_map(body, mesh=mesh, in_specs=placed, out_specs=P("ga", "gp"), check_vma=False)
```

profile of v0, /device:TPU:0, one launch (start us, length us, event | category | flops | bytes accessed | tf_op | source)
XLA Modules:
  0.0 658.7 jit_solution(5275239217300719659)
XLA Ops:
  6.5 0.0 copy-start
  6.5 0.0 all-reduce.3.cloned.1.call-start
  6.5 1.5 fusion.6
  11.9 10.0 %select_bitcast_fusion = (bf16[32,65536]{1,0:T(8,128)(2,1)}, bf16[32,65536]{1,0:T(8,128)(2,1)}, bf16[32,65536]{1,0:T(8,128)(2,1)}, bf16[32,65536]{1,0:T(8,128)(2...) fusion(bf16[1,32,65536]{2,1,0:T(8,128)(2,1)} %param.5, pred[]{:T(512)S(6)} %eq.23, pred[]{:T(512)S(6)} %eq.21, ...), kind=kLoop, calls=%fused_computation | loop fusion | flops 12582912 | bytes 29360134 | tf_op jit(solution)/shard_map/jit(_where)/select_n | solution.py:8
  21.9 0.0 all-reduce.3.cloned.1.call-update
  21.9 0.0 reduce-scatter.4.cloned.1.call-start
  22.0 399.9 %all-reduce.3.cloned.1.call-done = (bf16[32,65536]{1,0:T(8,128)(2,1)}, bf16[32,65536]{1,0:T(8,128)(2,1)}, bf16[32,65536]{1,0:T(8,128)(2,1)}, bf16[32,65536]{1,0:...) async-done(((bf16[32,65536]{1,0:T(8,128)(2,1)}, bf16[32,65536]{1,0:T(8,128)(2,1)}, bf16[32,65536]{1,0:T(8,128)(2,1)}, bf16[32,65536]{1,0:T(8,128)(2,1)}, ...) | async-done | bytes 25165840 | tf_op jit(solution)/shard_map/psum | solution.py:9
  421.9 0.0 copy-start.3
  421.9 16.2 %fusion.5 = f32[256,192]{0,1:T(8,128)S(1)} fusion(bf16[32,65536]{1,0:T(8,128)(2,1)} %get-tuple-element.5, bf16[256,65536]{1,0:T(8,128)(2,1)} %param.4), kind=kOutput, calls=%fused_computation.18 | convolution fusion | flops 1073741824 | bytes 37781504 | tf_op jit(solution)/shard_map/dot_general | solution.py:18
  438.1 0.0 copy-done.3
  438.1 15.0 %fusion.4 = f32[256,192]{0,1:T(8,128)S(1)} fusion(f32[256,192]{0,1:T(8,128)S(1)} %fusion.5, bf16[32,65536]{1,0:T(8,128)(2,1)S(1)} %copy-done.3, bf16[256,65536]{1,0:T(8,128)(2,1)} %param.4), kind=kOutput, calls=%fused_computation.16 | convolution fusion | flops 1073741824 | bytes 37781504 | tf_op jit(solution)/shard_map/dot_general | solution.py:18
  453.1 0.0 copy-start.2
  453.1 16.2 %fusion.3 = f32[256,192]{0,1:T(8,128)S(1)} fusion(f32[256,192]{0,1:T(8,128)S(1)} %fusion.4, bf16[32,65536]{1,0:T(8,128)(2,1)} %get-tuple-element.7, bf16[256,65536]{1,0:T(8,128)(2,1)} %param.4), kind=kOutput, calls=%fused_computation.14 | convolution fusion | flops 1073741824 | bytes 37781504 | tf_op jit(solution)/shard_map/dot_general | solution.py:18
  469.4 0.0 copy-done.2
  469.4 15.0 %fusion.2 = f32[256,192]{0,1:T(8,128)S(1)} fusion(f32[256,192]{0,1:T(8,128)S(1)} %fusion.3, bf16[32,65536]{1,0:T(8,128)(2,1)S(1)} %copy-done.2, bf16[256,65536]{1,0:T(8,128)(2,1)} %param.4), kind=kOutput, calls=%fused_computation.12 | convolution fusion | flops 1073741824 | bytes 37781504 | tf_op jit(solution)/shard_map/dot_general | solution.py:18
  484.4 0.0 copy-start.1
  484.4 16.2 %fusion.1 = f32[256,192]{0,1:T(8,128)S(1)} fusion(f32[256,192]{0,1:T(8,128)S(1)} %fusion.2, bf16[32,65536]{1,0:T(8,128)(2,1)} %get-tuple-element.9, bf16[256,65536]{1,0:T(8,128)(2,1)} %param.4), kind=kOutput, calls=%fused_computation.10 | convolution fusion | flops 1073741824 | bytes 37781504 | tf_op jit(solution)/shard_map/dot_general | solution.py:18
  500.7 0.0 copy-done.1
  500.7 15.0 %fusion = f32[256,192]{0,1:T(8,128)S(1)} fusion(f32[256,192]{0,1:T(8,128)S(1)} %fusion.1, bf16[32,65536]{1,0:T(8,128)(2,1)S(1)} %copy-done.1, bf16[256,65536]{1,0:T(8,128)(2,1)} %param.4), kind=kOutput, calls=%fused_computation.8 | convolution fusion | flops 1073741824 | bytes 37781504 | tf_op jit(solution)/shard_map/dot_general | solution.py:18
  515.7 0.0 copy-done
  515.7 0.7 convolution_bitcast_fusion
  516.4 1.3 copy.7
  517.7 0.0 reduce-scatter.4.cloned.1.call-update
  517.7 134.2 %reduce-scatter.4.cloned.1.call-done = f32[32,192]{1,0:T(8,128)} async-done(((f32[1024,192]{1,0:T(8,128)}), f32[32,192]{1,0:T(8,128)}) %reduce-scatter.4.cloned.1.call-update) | async-done | bytes 24592 | tf_op jit(solution)/shard_map/reduce_scatter | solution.py:23
Async XLA Ops:
  6.5 509.2 %copy-start = (bf16[1024,256]{1,0:T(8,128)(2,1)S(1)}, bf16[1024,256]{1,0:T(8,128)(2,1)}, u32[]{:S(2)}) copy-start(bf16[1024,256]{1,0:T(8,128)(2,1)} %param.6) | copy-start | bytes 1572868
  6.5 415.3 %all-reduce.3.cloned.1.call-start = ((), (), s32[]{:S(2)}) async-start(), calls=%async_computation.2 | async-start | bytes 50331648 | tf_op jit(solution)/shard_map/psum | solution.py:9
  21.9 629.9 %reduce-scatter.4.cloned.1.call-start = ((), (), s32[]{:S(2)}) async-start(), calls=%async_computation.1 | async-start | bytes 1081344 | tf_op jit(solution)/shard_map/reduce_scatter | solution.py:23
  421.9 16.2 %copy-start.3 = (bf16[32,65536]{1,0:T(8,128)(2,1)S(1)}, bf16[32,65536]{1,0:T(8,128)(2,1)}, u32[]{:S(2)}) copy-start(bf16[32,65536]{1,0:T(8,128)(2,1)} %get-tuple-element.6) | copy-start | bytes 12582916
  453.1 16.3 %copy-start.2 = (bf16[32,65536]{1,0:T(8,128)(2,1)S(1)}, bf16[32,65536]{1,0:T(8,128)(2,1)}, u32[]{:S(2)}) copy-start(bf16[32,65536]{1,0:T(8,128)(2,1)} %get-tuple-element.8) | copy-start | bytes 12582916
  484.4 16.3 %copy-start.1 = (bf16[32,65536]{1,0:T(8,128)(2,1)S(1)}, bf16[32,65536]{1,0:T(8,128)(2,1)}, u32[]{:S(2)}) copy-start(bf16[32,65536]{1,0:T(8,128)(2,1)} %get-tuple-element.10) | copy-start | bytes 12582916
Sparse Core Ops, SparseCore 0:
  22.1 399.7 all-reduce.2
  517.8 133.9 reduce-scatter.3
where the time goes:
time: 659 us
  waiting for transfers between devices  534 us (81%)
  matrix products  94.4 us (14%)
  between operations  17.4 us (3%)
  other arithmetic  9.97 us (2%)
    psum x1, waiting for transfers between devices, spread(): return lax.psum(block, axis)  400 us
    reduce_scatter x1, waiting for transfers between devices, body(): kernel = lax.psum_scatter(columns, 'ga', scatter_dimension=0, tiled=True)  134 us
    dot_general x6, matrix products, body(): lax.dot_general(screened, chosen, dims, preferred_element_type=jnp.float32)  93.7 us
  transfers between devices with their start and end apart: 2, of which 2 were waited for; matrix products, arithmetic and copies ran while one was open for 0% of the time, Pallas kernels for 0%

commit v1 on v0

v1 whole, which is shorter than its diff:
```python
import functools

import jax
import jax.numpy as jnp
from jax import lax
from jax.experimental import pallas as pl
from jax.experimental.pallas import tpu as pltpu
from jax.sharding import PartitionSpec as P

WIDTH = 512
PLANE = 8
PLANES = 4
LAG = 2


def remote(src, dst, send, recv, target):
    copy = pltpu.make_async_remote_copy(
        src_ref=src, dst_ref=dst, send_sem=send, recv_sem=recv,
        device_id={"ga": target}, device_id_type=pl.DeviceIdType.MESH)
    copy.start()


def drain(ref, sem):
    pltpu.make_async_copy(ref, ref, sem).wait()


def kernel(chunks, weight, valence, screened, conduction, out,
           slots, own, below, above, chosen, panel, acc, term, sum_core, recv_core, recv_plane, sum_plane, recv_line,
           spread_send, spread_recv, up_send, up_recv, down_send, down_recv, gather_send, across_x, across_y, corner,
           partner_recv, panel_sem, core_sem, plane_send, plane_recv, line_send, line_recv):
    rows = chosen.shape[2]
    half = rows // 2
    nb = weight.shape[0]
    nv = valence.shape[0]
    me = lax.axis_index("ga")
    z = me // PLANE
    j = lax.rem(me, PLANE)
    y = j // 4
    x = lax.rem(j // 2, 2)
    c = lax.rem(j, 2)
    base = z * PLANE
    jx = y * 4 + (1 - x) * 2 + c
    jy = (1 - y) * 4 + x * 2 + c
    jd = (1 - y) * 4 + (1 - x) * 2 + c
    jp = y * 4 + x * 2 + (1 - c)

    barrier = pltpu.get_barrier_semaphore()
    for step in range(1, PLANE):
        pl.semaphore_signal(barrier, inc=1, device_id={"ga": base + lax.rem(j + step, PLANE)}, device_id_type=pl.DeviceIdType.MESH)
    for step in range(1, PLANES):
        pl.semaphore_signal(barrier, inc=1, device_id={"ga": lax.rem(z + step, PLANES) * PLANE + j}, device_id_type=pl.DeviceIdType.MESH)
    pl.semaphore_wait(barrier, PLANE + PLANES - 2)

    def columns(t, piece):
        return pl.ds(pl.multiple_of((t * PLANE + piece) * WIDTH, WIDTH), WIDTH)

    def load_panel(t):
        wide = pl.ds(pl.multiple_of(t * PLANE * WIDTH, WIDTH), PLANE * WIDTH)
        slot = lax.rem(t, 2)
        return pltpu.make_async_copy(screened.at[:, wide], panel.at[slot], panel_sem.at[slot])

    def spread(t, carry):
        pltpu.make_async_copy(valence.at[:, columns(t, j)], slots.at[t, j], spread_recv.at[t]).start()
        for step in range(1, PLANE):
            piece = lax.rem(j + step, PLANE)
            remote(valence.at[:, columns(t, piece)], slots.at[t, j], spread_send.at[t], spread_recv.at[t], base + piece)
        return carry

    lax.fori_loop(0, chunks, spread, 0)
    load_panel(0).start()
    load_panel(1).start()
    acc[...] = jnp.zeros_like(acc)

    def pick(t):
        drain(slots.at[t], spread_recv.at[t])
        for b in range(nb):
            value = weight[b, 0] * slots[t, 0].astype(jnp.float32)
            for s in range(1, PLANE):
                value += weight[b, s] * slots[t, s].astype(jnp.float32)
            own[t, b * nv:(b + 1) * nv, :] = value.astype(jnp.bfloat16)

        @pl.when(z == 0)
        def _():
            remote(own.at[t], below.at[t], up_send.at[t], up_recv.at[t], me + PLANE)

        @pl.when(z == PLANES - 1)
        def _():
            remote(own.at[t], above.at[t], down_send.at[t], down_recv.at[t], me - PLANE)

        @pl.when(z == 1)
        def _():
            drain(below.at[t], up_recv.at[t])
            below[t] = below[t] + own[t]
            remote(below.at[t], below.at[t], up_send.at[t], up_recv.at[t], me + PLANE)

        @pl.when(z == 2)
        def _():
            drain(above.at[t], down_recv.at[t])
            above[t] = above[t] + own[t]
            remote(above.at[t], above.at[t], down_send.at[t], down_recv.at[t], me - PLANE)

    def total(t):
        @pl.when(z == 0)
        def _():
            drain(above.at[t], down_recv.at[t])
            chosen[t, j] = own[t] + above[t]

        @pl.when(z == PLANES - 1)
        def _():
            drain(below.at[t], up_recv.at[t])
            chosen[t, j] = own[t] + below[t]

        @pl.when(z == 1)
        def _():
            drain(above.at[t], down_recv.at[t])
            chosen[t, j] = below[t] + above[t]
            above[t] = above[t] + own[t]
            remote(above.at[t], above.at[t], down_send.at[t], down_recv.at[t], me - PLANE)

        @pl.when(z == 2)
        def _():
            drain(below.at[t], up_recv.at[t])
            chosen[t, j] = below[t] + above[t]
            below[t] = below[t] + own[t]
            remote(below.at[t], below.at[t], up_send.at[t], up_recv.at[t], me + PLANE)

        block = chosen.at[t, j]
        remote(block, block, gather_send.at[t], across_x.at[t], base + jx)
        remote(block, block, gather_send.at[t], across_y.at[t], base + jy)
        remote(block, block, gather_send.at[t], partner_recv.at[t], base + jp)

    def relay(t):
        drain(chosen.at[t, jx], across_x.at[t])
        late = chosen.at[t, jx, pl.ds(half, half)]
        remote(late, late, gather_send.at[t], corner.at[t], base + jy)
        drain(chosen.at[t, jy], across_y.at[t])
        early = chosen.at[t, jy, pl.ds(0, half)]
        remote(early, early, gather_send.at[t], corner.at[t], base + jx)
        for piece in (jx, jy):
            block = chosen.at[t, piece]
            remote(block, block, gather_send.at[t], partner_recv.at[t], base + jp)

    def last(t):
        drain(chosen.at[t, jd], corner.at[t])
        block = chosen.at[t, jd]
        remote(block, block, gather_send.at[t], partner_recv.at[t], base + jp)

    dims = (((1,), (1,)), ((), ()))

    def multiply(t):
        drain(chosen.at[t, pl.ds(0, 4)], partner_recv.at[t])
        load_panel(t).wait()
        slot = lax.rem(t, 2)
        value = acc[...]
        for piece in range(PLANE):
            value += lax.dot_general(panel[slot, :, piece * WIDTH:(piece + 1) * WIDTH], chosen[t, piece], dims,
                                     preferred_element_type=jnp.float32)
        acc[...] = value

        @pl.when(t + 2 < chunks)
        def _():
            load_panel(t + 2).start()

    shift = jnp.where((z == 0) | (z == PLANES - 1), 2, 0)

    def stage(t, action):
        @pl.when((t >= 0) & (t < chunks))
        def _():
            action(t)

    def turn(t, carry):
        stage(t, pick)
        u = t - LAG - shift
        stage(u, total)
        stage(u - LAG, relay)
        stage(u - 2 * LAG, last)
        stage(u - 3 * LAG, multiply)
        return carry

    lax.fori_loop(0, chunks + 4 * LAG + 2, turn, 0)

    value = acc[...]
    high = value.astype(jnp.bfloat16)
    rest = value - high.astype(jnp.float32)
    middle = rest.astype(jnp.bfloat16)
    low = (rest - middle.astype(jnp.float32)).astype(jnp.bfloat16)
    group = term.shape[2]
    per = 2 * group
    for k in range(term.shape[0]):
        left = conduction[k * per:(k + 1) * per, :]
        block = jnp.dot(left, low, preferred_element_type=jnp.float32)
        block += jnp.dot(left, middle, preferred_element_type=jnp.float32)
        block += jnp.dot(left, high, preferred_element_type=jnp.float32)
        term[k, 0] = block[:group]
        term[k, 1] = block[group:]

    remote(term.at[:, 1 - c], recv_core, core_sem.at[0], core_sem.at[1], base + jp)
    drain(recv_core, core_sem.at[1])
    for k in range(term.shape[0]):
        sum_core[k // 4, k % 4] = term[k, c] + recv_core[k]

    flips = (y * 2 + 1 - x, (1 - y) * 2 + x, (1 - y) * 2 + 1 - x)
    for r, chip in enumerate(flips):
        remote(sum_core.at[:, chip], recv_plane.at[r], plane_send.at[r], plane_recv.at[r], base + chip * 2 + c)
    for r in range(3):
        drain(recv_plane.at[r], plane_recv.at[r])
    mine = y * 2 + x
    for k in range(PLANES):
        sum_plane[k] = (sum_core[k, mine] + recv_plane[0, k]) + (recv_plane[1, k] + recv_plane[2, k])

    for d in range(1, PLANES):
        other = lax.rem(z + d, PLANES)
        remote(sum_plane.at[other], recv_line.at[d - 1], line_send.at[d - 1], line_recv.at[d - 1], other * PLANE + j)
    for d in range(PLANES - 1):
        drain(recv_line.at[d], line_recv.at[d])
    out[...] = (sum_plane[z] + recv_line[0]) + (recv_line[1] + recv_line[2])

    drain(recv_core, core_sem.at[0])
    for r in range(3):
        drain(recv_plane.at[r], plane_send.at[r])
        drain(recv_line.at[r], line_send.at[r])

    def finish(t, carry):
        drain(slots.at[t, pl.ds(0, PLANE - 1)], spread_send.at[t])
        drain(chosen.at[t, pl.ds(0, PLANE - 1)], gather_send.at[t])

        @pl.when(z < PLANES - 1)
        def _():
            drain(below.at[t], up_send.at[t])

        @pl.when(z > 0)
        def _():
            drain(above.at[t], down_send.at[t])

        return carry

    lax.fori_loop(0, chunks, finish, 0)


def fused(screened, valence, conduction, owner):
    own_slot = valence[0]
    nv, ng = own_slot.shape
    nb = owner.shape[0]
    rows = nb * nv
    chunks = ng // (PLANE * WIDTH)
    nc = conduction.shape[0]
    mine = nc // (PLANE * PLANES)
    plane = lax.axis_index("ga") // PLANE
    weight = (owner[:, None] == plane * PLANE + jnp.arange(PLANE)[None, :]).astype(jnp.float32)
    bf16, f32 = jnp.bfloat16, jnp.float32
    dma = pltpu.SemaphoreType.DMA
    line = pltpu.VMEM((chunks, rows, WIDTH), bf16)
    vmem = pl.BlockSpec(memory_space=pltpu.VMEM)
    anyspace = pl.BlockSpec(memory_space=pl.ANY)
    return pl.pallas_call(
        functools.partial(kernel, chunks),
        out_shape=jax.ShapeDtypeStruct((mine, rows), f32),
        in_specs=[pl.BlockSpec(memory_space=pltpu.SMEM), anyspace, anyspace, vmem],
        out_specs=vmem,
        scratch_shapes=[
            pltpu.VMEM((chunks, PLANE, nv, WIDTH), bf16),
            line, line, line,
            pltpu.VMEM((chunks, PLANE, rows, WIDTH), bf16),
            pltpu.VMEM((2, screened.shape[0], PLANE * WIDTH), bf16),
            pltpu.VMEM((screened.shape[0], rows), f32),
            pltpu.VMEM((PLANE * PLANES // 2, 2, mine, rows), f32),
            pltpu.VMEM((PLANES, 4, mine, rows), f32),
            pltpu.VMEM((PLANE * PLANES // 2, mine, rows), f32),
            pltpu.VMEM((3, PLANES, mine, rows), f32),
            pltpu.VMEM((PLANES, mine, rows), f32),
            pltpu.VMEM((3, mine, rows), f32),
        ] + [dma((chunks,))] * 11 + [dma((2,))] * 2 + [dma((3,))] * 4,
        compiler_params=pltpu.CompilerParams(collective_id=0, has_side_effects=True, vmem_limit_bytes=58 * 2**20),
        cost_estimate=pl.CostEstimate(flops=2 * screened.shape[0] * ng * rows, bytes_accessed=2 * screened.size, transcendentals=0),
    )(weight, own_slot, screened, conduction)


def spread_batch(block, axis, source):
    block = jnp.where(lax.axis_index(axis) == source, block, jnp.zeros_like(block))
    return lax.psum(block, axis)


def general(screened, valence, conduction, owner):
    own_slot = valence[0]
    dims = (((1,), (1,)), ((), ()))
    pieces = []
    for batch in range(owner.shape[0]):
        chosen = spread_batch(own_slot, "ga", owner[batch])
        pieces.append(lax.dot_general(screened, chosen, dims, preferred_element_type=jnp.float32))
    partial_value = jnp.concatenate(pieces, axis=1)
    cond_full = conduction.astype(jnp.float32)
    term = jnp.dot(cond_full, partial_value, precision=lax.Precision.HIGHEST)
    columns = lax.psum_scatter(term, "gp", scatter_dimension=1, tiled=True)
    return lax.psum_scatter(columns, "ga", scatter_dimension=0, tiled=True)


def solution(mesh):
    placed = (P("ga", "gp"), P("ga", None, "gp"), P(None, "ga"), P())
    body = fused if mesh.shape["ga"] == PLANE * PLANES and mesh.shape["gp"] == 1 else general
    return jax.shard_map(body, mesh=mesh, in_specs=placed, out_specs=P("ga", "gp"), check_vma=False)
```

time: 659 us -> 178 us (0.27)
  waiting for transfers between devices: 534 us -> 0 us
  Pallas kernels: 0 us -> 175 us
  matrix products: 94.4 us -> 0 us
  between operations: 17.4 us -> 0.01 us
  other arithmetic: 9.97 us -> 1.32 us
    psum x1 -> x0, waiting for transfers between devices: 400 us -> none  [spread(): return lax.psum(block, axis)]
    pallas_call x0 -> x1, Pallas kernels: none -> 175 us  [fused(): pl.pallas_call(functools.partial(kernel, chunks), out_shape=jax.ShapeDtyp...]
    reduce_scatter x1 -> x0, waiting for transfers between devices: 134 us -> none  [body(): kernel = lax.psum_scatter(columns, 'ga', scatter_dimension=0, tiled=True)]
    dot_general x7 -> x0, matrix products: 94.4 us -> none  [the longest x6 93.7 us: body(): lax.dot_general(screened, chosen, dims, preferred_element_type=jnp.float32)]
    select_n x1 -> x0, other arithmetic: 9.97 us -> none  [spread(): jnp.where(lax.axis_index(axis) == source, block, jnp.zeros_like(block))]
  transfers between devices with their start and end apart: 2 -> 0, of which waited for: 2 -> 0; matrix products, arithmetic and copies ran while one was open for 0% -> 0% of each run, Pallas kernels for 0% -> 0%
where the time goes in v1:
time: 178 us
  Pallas kernels  175 us (98%)
    pallas_call x1, Pallas kernels, fused(): pl.pallas_call(functools.partial(kernel, chunks), out_shape=jax.ShapeDtyp...  175 us

profile of v1, /device:TPU:0, one launch (start us, length us, event | category | flops | bytes accessed | tf_op | source)
XLA Modules:
  0.0 177.7 jit_solution(15511139159455648170)
XLA Ops:
  0.0 1.3 compare_convert_fusion.weight
  1.3 175.0 %shard_map.46 = f32[32,192]{1,0:T(8,128)} custom-call(f32[6,8]{1,0:T(8,128)} %compare_convert_fusion.weight, bf16[32,65536]{1,0:T(8,128)(2,1)} %bitcast.1, bf16[256,65536]{1,0:T(8,128)(2,1)} %screened.1, bf16[1024,256]{1,0:T(8,128)(2,1)} %conduction.1), custom_call_target="tpu_custom_call" | custom-call | flops 6442450944 | bytes 33554432 | tf_op jit(solution)/shard_map/pallas_call | solution.py:255
  176.4 1.4 copy.6
  (1 shorter events, 0.0 us)

commit v2 on v1

--- a/solution.py
+++ b/solution.py
@@ -27,9 +27,10 @@
 def kernel(chunks, weight, valence, screened, conduction, out,
            slots, own, below, above, chosen, panel, acc, term, sum_core, recv_core, recv_plane, sum_plane, recv_line,
            spread_send, spread_recv, up_send, up_recv, down_send, down_recv, gather_send, across_x, across_y, corner,
-           partner_recv, panel_sem, core_sem, plane_send, plane_recv, line_send, line_recv):
+           pair_recv, partner_recv, panel_sem, core_sem, plane_send, plane_recv, line_send, line_recv):
     rows = chosen.shape[2]
     half = rows // 2
+    quarter = half // 2
     nb = weight.shape[0]
     nv = valence.shape[0]
     me = lax.axis_index("ga")
@@ -43,6 +44,9 @@
     jy = (1 - y) * 4 + x * 2 + c
     jd = (1 - y) * 4 + (1 - x) * 2 + c
     jp = y * 4 + x * 2 + (1 - c)
+    odd = lax.rem(z, 2)
+    first = odd * half
+    pair = me + PLANE - 2 * PLANE * odd
 
     barrier = pltpu.get_barrier_semaphore()
     for step in range(1, PLANE):
@@ -131,17 +135,22 @@
 
     def relay(t):
         drain(chosen.at[t, jx], across_x.at[t])
-        late = chosen.at[t, jx, pl.ds(half, half)]
+        late = chosen.at[t, jx, pl.ds(pl.multiple_of(first + quarter, 16), quarter)]
         remote(late, late, gather_send.at[t], corner.at[t], base + jy)
         drain(chosen.at[t, jy], across_y.at[t])
-        early = chosen.at[t, jy, pl.ds(0, half)]
+        early = chosen.at[t, jy, pl.ds(pl.multiple_of(first, 16), quarter)]
         remote(early, early, gather_send.at[t], corner.at[t], base + jx)
         for piece in (jx, jy):
             block = chosen.at[t, piece]
             remote(block, block, gather_send.at[t], partner_recv.at[t], base + jp)
 
+    def swap(t):
+        drain(chosen.at[t, jd, pl.ds(0, half)], corner.at[t])
+        share = chosen.at[t, jd, pl.ds(pl.multiple_of(first, 16), half)]
+        remote(share, share, gather_send.at[t], pair_recv.at[t], pair)
+
     def last(t):
-        drain(chosen.at[t, jd], corner.at[t])
+        drain(chosen.at[t, jd, pl.ds(0, half)], pair_recv.at[t])
         block = chosen.at[t, jd]
         remote(block, block, gather_send.at[t], partner_recv.at[t], base + jp)
 
@@ -173,11 +182,12 @@
         u = t - LAG - shift
         stage(u, total)
         stage(u - LAG, relay)
-        stage(u - 2 * LAG, last)
-        stage(u - 3 * LAG, multiply)
+        stage(u - 2 * LAG, swap)
+        stage(u - 4 * LAG, last)
+        stage(u - 5 * LAG, multiply)
         return carry
 
-    lax.fori_loop(0, chunks + 4 * LAG + 2, turn, 0)
+    lax.fori_loop(0, chunks + 6 * LAG + 2, turn, 0)
 
     value = acc[...]
     high = value.astype(jnp.bfloat16)
@@ -269,7 +279,7 @@
             pltpu.VMEM((3, PLANES, mine, rows), f32),
             pltpu.VMEM((PLANES, mine, rows), f32),
             pltpu.VMEM((3, mine, rows), f32),
-        ] + [dma((chunks,))] * 11 + [dma((2,))] * 2 + [dma((3,))] * 4,
+        ] + [dma((chunks,))] * 12 + [dma((2,))] * 2 + [dma((3,))] * 4,
         compiler_params=pltpu.CompilerParams(collective_id=0, has_side_effects=True, vmem_limit_bytes=58 * 2**20),
         cost_estimate=pl.CostEstimate(flops=2 * screened.shape[0] * ng * rows, bytes_accessed=2 * screened.size, transcendentals=0),
     )(weight, own_slot, screened, conduction)

time: 178 us -> 175 us (0.983)
  Pallas kernels: 175 us -> 172 us
    pallas_call x1, Pallas kernels: 175 us -> 172 us  [fused(): pl.pallas_call(functools.partial(kernel, chunks), out_shape=jax.ShapeDtyp...]
where the time goes in v2:
time: 175 us
  Pallas kernels  172 us (98%)
    pallas_call x1, Pallas kernels, fused(): pl.pallas_call(functools.partial(kernel, chunks), out_shape=jax.ShapeDtyp...  172 us

profile of v2, /device:TPU:0, one launch (start us, length us, event | category | flops | bytes accessed | tf_op | source)
XLA Modules:
  0.0 174.9 jit_solution(7935491244206890429)
XLA Ops:
  0.0 1.3 compare_convert_fusion.weight
  1.3 172.2 %shard_map.46 = f32[32,192]{1,0:T(8,128)} custom-call(f32[6,8]{1,0:T(8,128)} %compare_convert_fusion.weight, bf16[32,65536]{1,0:T(8,128)(2,1)} %bitcast.1, bf16[256,65536]{1,0:T(8,128)(2,1)} %screened.1, bf16[1024,256]{1,0:T(8,128)(2,1)} %conduction.1), custom_call_target="tpu_custom_call" | custom-call | flops 6442450944 | bytes 33554432 | tf_op jit(solution)/shard_map/pallas_call | solution.py:265
  173.5 1.4 copy.6
  (1 shorter events, 0.0 us)
